TPU v7x, 32 devices: a whole 2x2x4 slice. The times are simulated.
32 devices in a mesh: depth: 4 (over y, x), probe: 8 (over z, core).
Axes of the slice: x: 2, y: 2, z: 4, core: 2. Of those that a mesh axis runs over, the one named last changes fastest.
Arguments:
- atom_blocks: bfloat16 [4, 1024, 128, 128], P('depth', 'probe'), may hold values from 0 to 1.5
- atom_tile: int32 [4, 1024], P('depth', 'probe'), may hold values from 0 to 255, as said below
- slice_counts: int32 [4], P('depth'), may hold values from 1 to 4, as said below
- positions: int32 [32], P('probe'), may hold values from 0 to 7, as said below
- probe_wave: float32 [2, 256, 256], replicated, may hold values from -4 to 4
- prop_phase: float32 [256, 256], replicated, may hold values from -3.140625 to 3.140625
Outputs:
- exit_waves: float32 [4, 32, 2, 256, 256], P('depth', 'probe')
Inputs may be any that keep to these rules, and one draw needn't show every extreme that they name: `atom_tile`: tile number owner * 32 + s * 8 + c names tile row owner, slice slot s and tile column c, with s below slice_counts of that section. In each section the 128 atoms of one index of probe (aligned blocks) name at most 24 tiles of any one tile row, and in every draw each section has a tile row that receives exactly 24 from every such block. `slice_counts`: some section has exactly 4 slices in every draw. The 4 probes of one tile row (aligned blocks of 4) have distinct positions.
All inputs are finite; a program needn't handle non-finite values.
Results may differ from a plain program's by a relative error of at most 0.04.
Values may be sent and summed in bfloat16 or wider, within the bound.
A program may use at most 128 MiB of HBM per device.

v0:
```python
import functools
import math

import jax
import jax.numpy as jnp
from jax import lax
from jax.experimental import pallas as pl
from jax.experimental.pallas import tpu as pltpu
from jax.sharding import PartitionSpec as P

SLICE_MAX = 4
TCOLS = 8


SIGMA = 0.7
PERIOD = 2.0 * math.pi / SIGMA
VMEM_LIMIT = 48 * 1024 * 1024


def reduced(value):
    return value - PERIOD * jnp.round(value * (1.0 / PERIOD))


def dft_tables(points):
    grid_index = jnp.arange(points, dtype=jnp.int32)
    angle_table = (grid_index[:, None] * grid_index[None, :] % points).astype(jnp.float32) * (
        2.0 * math.pi / points
    )
    norm_scale = 1.0 / math.sqrt(points)
    real_part = (jnp.cos(angle_table) * norm_scale).astype(jnp.bfloat16)
    imag_part = (-jnp.sin(angle_table) * norm_scale).astype(jnp.bfloat16)
    return (real_part, imag_part)


def rotor(phase):
    half = 0.5 * phase
    sq = half * half
    sine = half * (
        1.0
        + sq * (-1.0 / 6 + sq * (1.0 / 120 + sq * (-1.0 / 5040 + sq * (1.0 / 362880 - sq / 39916800.0))))
    )
    cosine = 1.0 + sq * (
        -0.5
        + sq
        * (1.0 / 24 + sq * (-1.0 / 720 + sq * (1.0 / 40320 + sq * (-1.0 / 3628800 + sq / 479001600.0))))
    )
    return 1.0 - 2.0 * sine * sine, 2.0 * sine * cosine


def sum_kernel(dests, tiles_dev, where_ref, mine_ref, own_ref, other_ref, kept_ref, sent_ref, total):
    total[...] = jnp.zeros_like(total)
    count = own_ref.shape[0]

    def add_from(ref, base):
        def body(atom, carry):
            place = where_ref[base + atom]

            @pl.when(place >= 0)
            def _():
                total[place] = total[place] + ref[atom].astype(jnp.float32)

            return carry

        lax.fori_loop(0, count, body, 0)

    add_from(own_ref, 0)
    add_from(other_ref, count)
    first = mine_ref[0] * tiles_dev

    def store_kept(tile, carry):
        kept_ref[tile] = total[first + tile]
        return carry

    lax.fori_loop(0, tiles_dev, store_kept, 0)

    def store_sent(tile, carry):
        sent_ref[tile] = reduced(total[tile]).astype(jnp.bfloat16)
        return carry

    lax.fori_loop(0, dests * tiles_dev, store_sent, 0)


def summed_atoms(where, mine, own, other, dests, tiles_dev):
    tile_size = own.shape[-1]
    rows = tile_size // 4
    smem = pl.BlockSpec(memory_space=pltpu.SMEM)

    def part(array_count):
        return pl.BlockSpec((array_count, rows, tile_size), lambda i: (0, i, 0))

    return pl.pallas_call(
        functools.partial(sum_kernel, dests, tiles_dev),
        grid=(tile_size // rows,),
        out_shape=(
            jax.ShapeDtypeStruct((tiles_dev, tile_size, tile_size), jnp.float32),
            jax.ShapeDtypeStruct((dests * tiles_dev, tile_size, tile_size), jnp.bfloat16),
        ),
        in_specs=[smem, smem, part(own.shape[0]), part(other.shape[0])],
        out_specs=(part(tiles_dev), part(dests * tiles_dev)),
        scratch_shapes=[pltpu.VMEM((dests * tiles_dev, rows, tile_size), jnp.float32)],
        compiler_params=pltpu.CompilerParams(vmem_limit_bytes=VMEM_LIMIT),
    )(where, mine, own, other)


def section_kernel(
    info,
    launched,
    carried,
    mid_a,
    mid_b,
    above_a,
    above_b,
    below_a,
    below_b,
    left,
    left_conj,
    right,
    right_conj,
    turn,
    former,
    result,
    leaving,
    wave,
):
    points = launched.shape[-1]
    active = info[0] > 0

    @pl.when(active)
    def _():
        @pl.when(info[1] > 0)
        def _():
            wave[...] = launched[...].reshape(2 * points, points)

        @pl.when(info[1] <= 0)
        def _():
            wave[...] = carried[...].reshape(2 * points, points).astype(jnp.float32)

        def right_apply(field, table):
            product = jnp.dot(field, table, preferred_element_type=jnp.float32)
            return (
                product[:points, :points] - product[points:, points:],
                product[:points, points:] + product[points:, :points],
            )

        def one_slice(s, carry):
            columns = [
                jnp.concatenate(
                    [above[s, 0].astype(jnp.float32), mid[s, 0], below[s, 0].astype(jnp.float32)],
                    axis=0,
                )
                for above, mid, below in ((above_a, mid_a, below_a), (above_b, mid_b, below_b))
            ]
            cosine, sine = rotor(SIGMA * jnp.concatenate(columns, axis=1))
            wave_re, wave_im = wave[:points], wave[points:]
            passed = jnp.concatenate(
                [wave_re * cosine - wave_im * sine, wave_re * sine + wave_im * cosine], axis=0
            ).astype(jnp.bfloat16)
            spectrum = jnp.dot(left[...], passed, preferred_element_type=jnp.float32)
            spec_re, spec_im = right_apply(spectrum.astype(jnp.bfloat16), right[...])
            turn_re, turn_im = turn[0], turn[1]
            propagated = jnp.concatenate(
                [spec_re * turn_re - spec_im * turn_im, spec_re * turn_im + spec_im * turn_re], axis=0
            ).astype(jnp.bfloat16)
            returned = jnp.dot(left_conj[...], propagated, preferred_element_type=jnp.float32)
            back_re, back_im = right_apply(returned.astype(jnp.bfloat16), right_conj[...])
            wave[:points] = back_re
            wave[points:] = back_im
            return carry

        lax.fori_loop(0, info[2], one_slice, 0)
        out = wave[...].reshape(2, points, points)
        result[0] = out
        leaving[...] = out.astype(jnp.bfloat16)

    @pl.when(jnp.logical_not(active))
    def _():
        result[...] = former[...]
        leaving[...] = jnp.zeros_like(leaving)


def run_section(info, launched, carried, mid, above, below, tables, results):
    points = launched.shape[-1]
    slots, _, tile_size, _ = mid.shape
    half = above.shape[2]

    def whole(array):
        return pl.BlockSpec(array.shape, lambda i, info, n=array.ndim: (0,) * n)

    def column(rows, which):
        return pl.BlockSpec((slots, 1, rows, tile_size), lambda i, info: (0, info[which], 0, 0))

    place = pl.BlockSpec((1, 2, points, points), lambda i, info: (info[5], 0, 0, 0))
    grid_spec = pltpu.PrefetchScalarGridSpec(
        num_scalar_prefetch=1,
        grid=(1,),
        in_specs=[
            whole(launched),
            whole(carried),
            column(tile_size, 3),
            column(tile_size, 4),
            column(half, 3),
            column(half, 4),
            column(half, 3),
            column(half, 4),
            *[whole(t) for t in tables],
            place,
        ],
        out_specs=[place, whole(carried)],
        scratch_shapes=[pltpu.VMEM((2 * points, points), jnp.float32)],
    )
    return pl.pallas_call(
        section_kernel,
        grid_spec=grid_spec,
        out_shape=[
            jax.ShapeDtypeStruct(results.shape, results.dtype),
            jax.ShapeDtypeStruct(carried.shape, carried.dtype),
        ],
        input_output_aliases={9 + len(tables): 0},
        compiler_params=pltpu.CompilerParams(vmem_limit_bytes=VMEM_LIMIT),
    )(info, launched, carried, mid, mid, above, above, below, below, *tables, results)


def shards(atom_blocks, atom_tile, slice_counts, positions, probe_wave, prop_phase):
    owners = lax.axis_size("probe")
    sections = lax.axis_size("depth")
    depth_index = lax.axis_index("depth")
    probe_index = lax.axis_index("probe")
    tile_size = atom_blocks.shape[-1]
    half_tile = tile_size // 2
    tiles_dev = SLICE_MAX * TCOLS
    pairs = owners // 2
    rank, core = probe_index // 2, probe_index % 2

    blocks, targets = atom_blocks[0], atom_tile[0]
    swap = [(i, i ^ 1) for i in range(owners)]
    other_blocks = lax.ppermute(blocks, "probe", swap)
    other_targets = lax.ppermute(targets, "probe", swap)
    named = jnp.concatenate([targets, other_targets])
    owner_of = named // tiles_dev
    where = jnp.where(owner_of % 2 == core, (owner_of // 2) * tiles_dev + named % tiles_dev, -1)
    kept, sent = summed_atoms(where, rank[None], blocks, other_blocks, pairs, tiles_dev)
    sent = sent.reshape(pairs, tiles_dev, tile_size, tile_size)

    up_in = down_in = None
    for step in range(pairs - 1):
        up_to = jnp.clip(pairs - 1 - step + rank, 0, pairs - 1)
        down_to = jnp.clip(step - (pairs - 1) + rank, 0, pairs - 1)
        up_out = lax.dynamic_index_in_dim(sent, up_to, 0, keepdims=False)
        down_out = lax.dynamic_index_in_dim(sent, down_to, 0, keepdims=False)
        if step:
            up_out = reduced(up_out.astype(jnp.float32) + up_in.astype(jnp.float32))
            down_out = reduced(down_out.astype(jnp.float32) + down_in.astype(jnp.float32))
            up_out, down_out = up_out.astype(jnp.bfloat16), down_out.astype(jnp.bfloat16)
        up_route, down_route = [], []
        for z in range(min(step + 1, pairs - 1)):
            for c in range(2):
                up_route.append((2 * z + c, 2 * (z + 1) + c))
                down_route.append((2 * (pairs - 1 - z) + c, 2 * (pairs - 2 - z) + c))
        up_in = lax.ppermute(up_out, "probe", up_route)
        down_in = lax.ppermute(down_out, "probe", down_route)
    if up_in is not None:
        kept = kept + up_in.astype(jnp.float32) + down_in.astype(jnp.float32)
    mid = reduced(kept).reshape(SLICE_MAX, TCOLS, tile_size, tile_size)
    narrow = mid.astype(jnp.bfloat16)
    up = [(i, (i + 1) % owners) for i in range(owners)]
    down = [(j, i) for i, j in up]
    above = lax.ppermute(narrow[:, :, half_tile:], "probe", up)
    below = lax.ppermute(narrow[:, :, :half_tile], "probe", down)

    real_part, imag_part = dft_tables(2 * tile_size)
    left = jnp.block([[real_part, -imag_part], [imag_part, real_part]])
    left_conj = jnp.block([[real_part, imag_part], [-imag_part, real_part]])
    right = jnp.concatenate([real_part, imag_part], axis=1)
    right_conj = jnp.concatenate([real_part, -imag_part], axis=1)
    turn = jnp.stack([jnp.cos(prop_phase), jnp.sin(prop_phase)])
    tables = (left, left_conj, right, right_conj, turn)

    waves_dev = positions.shape[0]
    results = jnp.zeros((waves_dev, *probe_wave.shape), jnp.float32)
    carried = jnp.zeros(probe_wave.shape, jnp.bfloat16)
    forward = [(d, d + 1) for d in range(sections - 1)]
    step_total = waves_dev + sections - 1
    for step in range(step_total):
        wave_index = step - depth_index
        active = (wave_index >= 0) & (wave_index < waves_dev)
        wave_index = jnp.clip(wave_index, 0, waves_dev - 1)
        column = positions[wave_index]
        info = jnp.stack(
            [
                active.astype(jnp.int32),
                (depth_index == 0).astype(jnp.int32),
                slice_counts[0],
                column,
                (column + 1) % TCOLS,
                wave_index,
            ]
        )
        results, leaving = run_section(
            info, probe_wave, carried, mid, above, below, tables, results
        )
        if step + 1 < step_total:
            carried = lax.ppermute(leaving, "depth", forward)
    return results[None]


def solution(mesh):
    in_specs = (
        P("depth", "probe", None, None),
        P("depth", "probe"),
        P("depth"),
        P("probe"),
        P(),
        P(),
    )
    out_specs = P("depth", "probe", None, None, None)
    return jax.shard_map(shards, mesh=mesh, in_specs=in_specs, out_specs=out_specs, check_vma=False)
```

profile of v0, /device:TPU:6, one launch (start us, length us, event | category | flops | bytes accessed | tf_op | source)
XLA Modules:
  0.0 284.4 jit_solution(13357104185164675823)
XLA Ops:
  0.5 5.5 %collective-permute-done = s32[128]{0:T(128)S(1)} collective-permute-done((s32[128]{0:T(128)}, s32[128]{0:T(128)S(1)}, u32[]{:S(2)}, u32[]{:S(2)}) %collective-permute-start) | collective-permute-done | bytes 544 | tf_op jit(solution)/shard_map/ppermute | solution.py:237
  7.5 23.6 %shard_map.64 = (f32[32,128,128]{2,1,0:T(8,128)S(1)}, bf16[128,128,128]{2,1,0:T(8,128)(2,1)}) custom-call(s32[256]{0:T(256)S(1)} %compare_select_fusion.where_ref, s32[1]{0:T(128)} %bitcast.30.mine_ref, bf16[128,128,128]{2,1,0:T(8,128)(2,1)} %bitcast.75, bf16[128,128,128]{2,1,0:T(8,128)(2,1)} %collective-permute-done.1.other_ref), custom_call_target="tpu_custom_call" | custom-call | tf_op jit(solution)/shard_map/pallas_call | solution.py:91
  33.8 4.5 %collective-permute-start.2 = (bf16[32,128,128]{2,1,0:T(8,128)(2,1)}, bf16[32,128,128]{2,1,0:T(8,128)(2,1)}, u32[]{:S(2)}, u32[]{:S(2)}) collective-permute-start(bf16[32,128,128]{2,1,0:T(8,128)(2,1)} %get-tuple-element.37), channel_id=1, source_target_pairs={{0,2},{1,3},{8,10},{9,11},{16,18},{17,19},{24,26},{25,27}} | collective-permute-start | bytes 3145736 | tf_op jit(solution)/shard_map/ppermute | solution.py:259
  40.0 20.4 %collective-permute-done.2 = bf16[32,128,128]{2,1,0:T(8,128)(2,1)} collective-permute-done((bf16[32,128,128]{2,1,0:T(8,128)(2,1)}, bf16[32,128,128]{2,1,0:T(8,128)(2,1)}, u32[]{:S(2)}, u32[]{:S(2)}) %collective-permute-start.2) | collective-permute-done | bytes 1048608 | tf_op jit(solution)/shard_map/ppermute | solution.py:259
  60.4 3.1 %subtract_convert_fusion.3 = bf16[32,128,128]{2,1,0:T(8,128)(2,1)} fusion(bf16[32,128,128]{2,1,0:T(8,128)(2,1)} %collective-permute-done.2, bf16[4,32,128,128]{3,2,1,0:T(8,128)(2,1)} %bitcast.71, s32[]{:T(128)S(6)} %min.48), kind=kLoop, calls=%fused_computation.8 | loop fusion | flops 4194304 | bytes 3145732 | tf_op jit(solution)/shard_map/convert_element_type | solution.py:253
  63.5 5.4 %collective-permute-start.3 = (bf16[32,128,128]{2,1,0:T(8,128)(2,1)}, bf16[32,128,128]{2,1,0:T(8,128)(2,1)}, u32[]{:S(2)}, u32[]{:S(2)}) collective-permute-start(bf16[32,128,128]{2,1,0:T(8,128)(2,1)} %subtract_convert_fusion.3), channel_id=1, source_target_pairs={{0,2},{1,3},{2,4},{3,5},{8,10},{9,11},{10,12},{11,13},{16,18},{17,... | collective-permute-start | bytes 3145736 | tf_op jit(solution)/shard_map/ppermute | solution.py:259
  68.8 21.3 %collective-permute-done.3 = bf16[32,128,128]{2,1,0:T(8,128)(2,1)} collective-permute-done((bf16[32,128,128]{2,1,0:T(8,128)(2,1)}, bf16[32,128,128]{2,1,0:T(8,128)(2,1)}, u32[]{:S(2)}, u32[]{:S(2)}) %collective-permute-start.3) | collective-permute-done | bytes 1048608 | tf_op jit(solution)/shard_map/ppermute | solution.py:259
  90.1 4.9 %subtract_convert_fusion.2 = (bf16[32,128,128]{2,1,0:T(8,128)(2,1)}, bf16[32,128,128]{2,1,0:T(8,128)(2,1)}) fusion(bf16[32,128,128]{2,1,0:T(8,128)(2,1)} %collective-permute-done.3, bf16[4,32,128,128]{3,2,1,0:T(8,128)(2,1)} %bitcast.72, s32[]{:T(128)S(6)} %min.47, bf16[32,128,128]{2,1,0:T(8,128)(2,1)} %collective-permute-done.5, s32[]{:T(128)S(6)} %min.51), kind=kLoop, calls=%fused_computation.7 | loop fusion | flops 8388608 | bytes 6291464 | tf_op jit(solution)/shard_map/convert_element_type | solution.py:253
  95.8 5.0 %collective-permute-start.4 = (bf16[32,128,128]{2,1,0:T(8,128)(2,1)}, bf16[32,128,128]{2,1,0:T(8,128)(2,1)S(1)}, u32[]{:S(2)}, u32[]{:S(2)}) collective-permute-start(bf16[32,128,128]{2,1,0:T(8,128)(2,1)} %get-tuple-element.35), channel_id=1, source_target_pairs={{0,2},{1,3},{2,4},{3,5},{4,6},{5,7},{8,10},{9,11},{10,12},{11,13},... | collective-permute-start | bytes 3145736 | tf_op jit(solution)/shard_map/ppermute | solution.py:259
  104.9 17.2 %collective-permute-done.4 = bf16[32,128,128]{2,1,0:T(8,128)(2,1)S(1)} collective-permute-done((bf16[32,128,128]{2,1,0:T(8,128)(2,1)}, bf16[32,128,128]{2,1,0:T(8,128)(2,1)S(1)}, u32[]{:S(2)}, u32[]{:S(2)}) %collective-permute-start.4) | collective-permute-done | bytes 1048608 | tf_op jit(solution)/shard_map/ppermute | solution.py:259
  122.1 25.6 %collective-permute-done.7 = bf16[32,128,128]{2,1,0:T(8,128)(2,1)S(1)} collective-permute-done((bf16[32,128,128]{2,1,0:T(8,128)(2,1)S(1)}, bf16[32,128,128]{2,1,0:T(8,128)(2,1)S(1)}, u32[]{:S(2)}, u32[]{:S(2)}) %collective-permute-start.7) | collective-permute-done | bytes 1048608 | tf_op jit(solution)/shard_map/ppermute | solution.py:260
  150.0 3.5 %collective-permute-start.9 = (bf16[4,8,64,128]{3,2,1,0:T(8,128)(2,1)}, bf16[4,8,64,128]{3,2,1,0:T(8,128)(2,1)S(1)}, u32[]{:S(2)}, u32[]{:S(2)}) collective-permute-start(bf16[4,8,64,128]{3,2,1,0:T(8,128)(2,1)} %get-tuple-element.39), channel_id=1, source_target_pairs={{1,0},{2,1},{3,2},{4,3},{5,4},{6,5},{7,6},{0,7},{9,8},{10,9},{11,1... | collective-permute-start | bytes 1572872 | tf_op jit(solution)/shard_map/ppermute | solution.py:268
  158.6 7.3 %collective-permute-done.8.above_a.above_b = bf16[4,8,64,128]{3,2,1,0:T(8,128)(2,1)S(1)} collective-permute-done((bf16[4,8,64,128]{3,2,1,0:T(8,128)(2,1)}, bf16[4,8,64,128]{3,2,1,0:T(8,128)(2,1)S(1)}, u32[]{:S(2)}, u32[]{:S(2)}) %collective-permute-start.8) | collective-permute-done | bytes 524320 | tf_op jit(solution)/shard_map/ppermute | solution.py:267
  172.7 8.1 %collective-permute-done.10.carried = bf16[2,256,256]{2,1,0:T(8,128)(2,1)} collective-permute-done((bf16[2,256,256]{2,1,0:T(8,128)(2,1)}, bf16[2,256,256]{2,1,0:T(8,128)(2,1)}, u32[]{:S(2)}, u32[]{:S(2)}) %collective-permute-start.10) | collective-permute-done | bytes 262176 | tf_op jit(solution)/shard_map/ppermute | solution.py:302
  187.2 7.0 %collective-permute-done.11.carried = bf16[2,256,256]{2,1,0:T(8,128)(2,1)} collective-permute-done((bf16[2,256,256]{2,1,0:T(8,128)(2,1)}, bf16[2,256,256]{2,1,0:T(8,128)(2,1)}, u32[]{:S(2)}, u32[]{:S(2)}) %collective-permute-start.11) | collective-permute-done | bytes 262176 | tf_op jit(solution)/shard_map/ppermute | solution.py:302
  195.2 2.8 shard_map.67
  200.6 20.1 %collective-permute-done.12.carried = bf16[2,256,256]{2,1,0:T(8,128)(2,1)} collective-permute-done((bf16[2,256,256]{2,1,0:T(8,128)(2,1)}, bf16[2,256,256]{2,1,0:T(8,128)(2,1)}, u32[]{:S(2)}, u32[]{:S(2)}) %collective-permute-start.12) | collective-permute-done | bytes 262176 | tf_op jit(solution)/shard_map/ppermute | solution.py:302
  221.6 7.6 %shard_map.68 = (f32[4,2,256,256]{3,2,1,0:T(8,128)}, bf16[2,256,256]{2,1,0:T(8,128)(2,1)}) custom-call(s32[6]{0:T(128)S(1)} %stack.147.info, f32[2,256,256]{2,1,0:T(8,128)S(1)} %copy-done, bf16[2,256,256]{2,1,0:T(8,128)(2,1)} %collective-permute-done.12.carried, f32[4,8,128,128]{3,2,1,0:T(8,128)} %bitcast.62, ...), custom_call_target="tpu_custom_call", output_to_operand_aliasing={{0}: (14, {})} | custom-call | tf_op jit(solution)/shard_map/pallas_call | solution.py:211
  232.0 7.1 %collective-permute-done.13.carried = bf16[2,256,256]{2,1,0:T(8,128)(2,1)} collective-permute-done((bf16[2,256,256]{2,1,0:T(8,128)(2,1)}, bf16[2,256,256]{2,1,0:T(8,128)(2,1)}, u32[]{:S(2)}, u32[]{:S(2)}) %collective-permute-start.13) | collective-permute-done | bytes 262176 | tf_op jit(solution)/shard_map/ppermute | solution.py:302
  240.0 7.6 %shard_map.69 = (f32[4,2,256,256]{3,2,1,0:T(8,128)}, bf16[2,256,256]{2,1,0:T(8,128)(2,1)}) custom-call(s32[6]{0:T(128)S(1)} %stack.142.info, f32[2,256,256]{2,1,0:T(8,128)S(1)} %copy-done, bf16[2,256,256]{2,1,0:T(8,128)(2,1)} %collective-permute-done.13.carried, f32[4,8,128,128]{3,2,1,0:T(8,128)} %bitcast.64, ...), custom_call_target="tpu_custom_call", output_to_operand_aliasing={{0}: (14, {})} | custom-call | tf_op jit(solution)/shard_map/pallas_call | solution.py:211
  250.4 6.8 %collective-permute-done.14.carried = bf16[2,256,256]{2,1,0:T(8,128)(2,1)} collective-permute-done((bf16[2,256,256]{2,1,0:T(8,128)(2,1)}, bf16[2,256,256]{2,1,0:T(8,128)(2,1)}, u32[]{:S(2)}, u32[]{:S(2)}) %collective-permute-start.14) | collective-permute-done | bytes 262176 | tf_op jit(solution)/shard_map/ppermute | solution.py:302
  258.2 7.6 %shard_map.70 = (f32[4,2,256,256]{3,2,1,0:T(8,128)}, bf16[2,256,256]{2,1,0:T(8,128)(2,1)}) custom-call(s32[6]{0:T(128)S(1)} %stack.137.info, f32[2,256,256]{2,1,0:T(8,128)S(1)} %copy-done, bf16[2,256,256]{2,1,0:T(8,128)(2,1)} %collective-permute-done.14.carried, f32[4,8,128,128]{3,2,1,0:T(8,128)} %bitcast.66, ...), custom_call_target="tpu_custom_call", output_to_operand_aliasing={{0}: (14, {})} | custom-call | tf_op jit(solution)/shard_map/pallas_call | solution.py:211
  268.4 7.5 %collective-permute-done.15.carried = bf16[2,256,256]{2,1,0:T(8,128)(2,1)} collective-permute-done((bf16[2,256,256]{2,1,0:T(8,128)(2,1)}, bf16[2,256,256]{2,1,0:T(8,128)(2,1)}, u32[]{:S(2)}, u32[]{:S(2)}) %collective-permute-start.15) | collective-permute-done | bytes 262176 | tf_op jit(solution)/shard_map/ppermute | solution.py:302
  276.9 7.6 %shard_map.71 = (f32[4,2,256,256]{3,2,1,0:T(8,128)}, bf16[2,256,256]{2,1,0:T(8,128)(2,1)}) custom-call(s32[6]{0:T(128)S(1)} %stack.132.info, f32[2,256,256]{2,1,0:T(8,128)S(1)} %copy-done, bf16[2,256,256]{2,1,0:T(8,128)(2,1)} %collective-permute-done.15.carried, f32[4,8,128,128]{3,2,1,0:T(8,128)} %bitcast.68, ...), custom_call_target="tpu_custom_call", output_to_operand_aliasing={{0}: (14, {})} | custom-call | tf_op jit(solution)/shard_map/pallas_call | solution.py:211
  (62 shorter events, 41.9 us)
Async XLA Ops:
  0.0 7.5 %collective-permute-start.1 = (bf16[128,128,128]{2,1,0:T(8,128)(2,1)}, bf16[128,128,128]{2,1,0:T(8,128)(2,1)}, u32[]{:S(2)}, u32[]{:S(2)}) collective-permute-start(bf16[128,128,128]{2,1,0:T(8,128)(2,1)} %bitcast.74), channel_id=1, source_target_pairs={{0,1},{1,0},{2,3},{3,2},{4,5},{5,4},{6,7},{7,6},{8,9},{9,8},{10,11... | collective-permute-start | bytes 12582920 | tf_op jit(solution)/shard_map/ppermute | solution.py:236
  0.0 6.0 %collective-permute-start = (s32[128]{0:T(128)}, s32[128]{0:T(128)S(1)}, u32[]{:S(2)}, u32[]{:S(2)}) collective-permute-start(s32[128]{0:T(128)} %bitcast.76), channel_id=1, source_target_pairs={{0,1},{1,0},{2,3},{3,2},{4,5},{5,4},{6,7},{7,6},{8,9},{9,8},{10,11... | collective-permute-start | bytes 1544 | tf_op jit(solution)/shard_map/ppermute | solution.py:237
  33.8 26.5 %collective-permute-start.2 = (bf16[32,128,128]{2,1,0:T(8,128)(2,1)}, bf16[32,128,128]{2,1,0:T(8,128)(2,1)}, u32[]{:S(2)}, u32[]{:S(2)}) collective-permute-start(bf16[32,128,128]{2,1,0:T(8,128)(2,1)} %get-tuple-element.37), channel_id=1, source_target_pairs={{0,2},{1,3},{8,10},{9,11},{16,18},{17,19},{24,26},{25,27}} | collective-permute-start | bytes 3145736 | tf_op jit(solution)/shard_map/ppermute | solution.py:259
  38.3 30.5 %collective-permute-start.5 = (bf16[32,128,128]{2,1,0:T(8,128)(2,1)S(1)}, bf16[32,128,128]{2,1,0:T(8,128)(2,1)}, u32[]{:S(2)}, u32[]{:S(2)}) collective-permute-start(bf16[32,128,128]{2,1,0:T(8,128)(2,1)S(1)} %get-tuple-element.38), channel_id=1, source_target_pairs={{6,4},{7,5},{14,12},{15,13},{22,20},{23,21},{30,28},{31,29}} | collective-permute-start | bytes 3145736 | tf_op jit(solution)/shard_map/ppermute | solution.py:260
  63.5 26.6 %collective-permute-start.3 = (bf16[32,128,128]{2,1,0:T(8,128)(2,1)}, bf16[32,128,128]{2,1,0:T(8,128)(2,1)}, u32[]{:S(2)}, u32[]{:S(2)}) collective-permute-start(bf16[32,128,128]{2,1,0:T(8,128)(2,1)} %subtract_convert_fusion.3), channel_id=1, source_target_pairs={{0,2},{1,3},{2,4},{3,5},{8,10},{9,11},{10,12},{11,13},{16,18},{17,... | collective-permute-start | bytes 3145736 | tf_op jit(solution)/shard_map/ppermute | solution.py:259
  95.0 9.0 %copy-start.9 = (f32[256,256]{1,0:T(8,128)S(1)}, f32[256,256]{1,0:T(8,128)}, u32[]{:S(2)}) copy-start(f32[256,256]{1,0:T(8,128)} %param.11) | copy-start | bytes 786436
  95.0 5.9 %collective-permute-start.6 = (bf16[32,128,128]{2,1,0:T(8,128)(2,1)}, bf16[32,128,128]{2,1,0:T(8,128)(2,1)S(1)}, u32[]{:S(2)}, u32[]{:S(2)}) collective-permute-start(bf16[32,128,128]{2,1,0:T(8,128)(2,1)} %get-tuple-element.36), channel_id=1, source_target_pairs={{6,4},{7,5},{4,2},{5,3},{14,12},{15,13},{12,10},{13,11},{22,20},{2... | collective-permute-start | bytes 3145736 | tf_op jit(solution)/shard_map/ppermute | solution.py:260
  95.8 26.3 %collective-permute-start.4 = (bf16[32,128,128]{2,1,0:T(8,128)(2,1)}, bf16[32,128,128]{2,1,0:T(8,128)(2,1)S(1)}, u32[]{:S(2)}, u32[]{:S(2)}) collective-permute-start(bf16[32,128,128]{2,1,0:T(8,128)(2,1)} %get-tuple-element.35), channel_id=1, source_target_pairs={{0,2},{1,3},{2,4},{3,5},{4,6},{5,7},{8,10},{9,11},{10,12},{11,13},... | collective-permute-start | bytes 3145736 | tf_op jit(solution)/shard_map/ppermute | solution.py:259
  102.7 45.1 %collective-permute-start.7 = (bf16[32,128,128]{2,1,0:T(8,128)(2,1)S(1)}, bf16[32,128,128]{2,1,0:T(8,128)(2,1)S(1)}, u32[]{:S(2)}, u32[]{:S(2)}) collective-permute-start(bf16[32,128,128]{2,1,0:T(8,128)(2,1)S(1)} %subtract_convert_fusion), channel_id=1, source_target_pairs={{6,4},{7,5},{4,2},{5,3},{2,0},{3,1},{14,12},{15,13},{12,10},{13,11... | collective-permute-start | bytes 3145736 | tf_op jit(solution)/shard_map/ppermute | solution.py:260
  148.3 1.7 copy-start.8
  148.3 6.2 %copy-start.10 = (s32[4]{0:T(128)S(1)}, s32[4]{0:T(128)}, u32[]{:S(2)}) copy-start(s32[4]{0:T(128)} %param.9) | copy-start | bytes 52
  150.0 15.9 %collective-permute-start.8 = (bf16[4,8,64,128]{3,2,1,0:T(8,128)(2,1)}, bf16[4,8,64,128]{3,2,1,0:T(8,128)(2,1)S(1)}, u32[]{:S(2)}, u32[]{:S(2)}) collective-permute-start(bf16[4,8,64,128]{3,2,1,0:T(8,128)(2,1)} %get-tuple-element.40), channel_id=1, source_target_pairs={{0,1},{1,2},{2,3},{3,4},{4,5},{5,6},{6,7},{7,0},{8,9},{9,10},{10,1... | collective-permute-start | bytes 1572872 | tf_op jit(solution)/shard_map/ppermute | solution.py:267
  150.0 15.9 %collective-permute-start.9 = (bf16[4,8,64,128]{3,2,1,0:T(8,128)(2,1)}, bf16[4,8,64,128]{3,2,1,0:T(8,128)(2,1)S(1)}, u32[]{:S(2)}, u32[]{:S(2)}) collective-permute-start(bf16[4,8,64,128]{3,2,1,0:T(8,128)(2,1)} %get-tuple-element.39), channel_id=1, source_target_pairs={{1,0},{2,1},{3,2},{4,3},{5,4},{6,5},{7,6},{0,7},{9,8},{10,9},{11,1... | collective-permute-start | bytes 1572872 | tf_op jit(solution)/shard_map/ppermute | solution.py:268
  158.5 11.7 %copy-start.1 = (bf16[256,512]{1,0:T(8,128)(2,1)}, bf16[256,512]{1,0:T(8,128)(2,1)S(1)}, u32[]{:S(2)}) copy-start(bf16[256,512]{1,0:T(8,128)(2,1)S(1)} %get-tuple-element.46.right) | copy-start | bytes 786436
  158.5 8.9 %copy-start = (f32[2,256,256]{2,1,0:T(8,128)S(1)}, f32[2,256,256]{2,1,0:T(8,128)}, u32[]{:S(2)}) copy-start(f32[2,256,256]{2,1,0:T(8,128)} %launched.13) | copy-start | bytes 1572868
  170.1 10.6 %collective-permute-start.10 = (bf16[2,256,256]{2,1,0:T(8,128)(2,1)}, bf16[2,256,256]{2,1,0:T(8,128)(2,1)}, u32[]{:S(2)}, u32[]{:S(2)}) collective-permute-start(bf16[2,256,256]{2,1,0:T(8,128)(2,1)} %get-tuple-element.22), channel_id=1, source_target_pairs={{0,8},{8,16},{16,24},{1,9},{9,17},{17,25},{2,10},{10,18},{18,26},{... | collective-permute-start | bytes 786440 | tf_op jit(solution)/shard_map/ppermute | solution.py:302
  180.8 1.0 copy-start.2
  184.5 9.8 %collective-permute-start.11 = (bf16[2,256,256]{2,1,0:T(8,128)(2,1)}, bf16[2,256,256]{2,1,0:T(8,128)(2,1)}, u32[]{:S(2)}, u32[]{:S(2)}) collective-permute-start(bf16[2,256,256]{2,1,0:T(8,128)(2,1)} %get-tuple-element.24), channel_id=1, source_target_pairs={{0,8},{8,16},{16,24},{1,9},{9,17},{17,25},{2,10},{10,18},{18,26},{... | collective-permute-start | bytes 786440 | tf_op jit(solution)/shard_map/ppermute | solution.py:302
  194.3 1.0 copy-start.3
  198.0 22.7 %collective-permute-start.12 = (bf16[2,256,256]{2,1,0:T(8,128)(2,1)}, bf16[2,256,256]{2,1,0:T(8,128)(2,1)}, u32[]{:S(2)}, u32[]{:S(2)}) collective-permute-start(bf16[2,256,256]{2,1,0:T(8,128)(2,1)} %get-tuple-element.26), channel_id=1, source_target_pairs={{0,8},{8,16},{16,24},{1,9},{9,17},{17,25},{2,10},{10,18},{18,26},{... | collective-permute-start | bytes 786440 | tf_op jit(solution)/shard_map/ppermute | solution.py:302
  220.7 1.0 copy-start.4
  229.2 9.9 %collective-permute-start.13 = (bf16[2,256,256]{2,1,0:T(8,128)(2,1)}, bf16[2,256,256]{2,1,0:T(8,128)(2,1)}, u32[]{:S(2)}, u32[]{:S(2)}) collective-permute-start(bf16[2,256,256]{2,1,0:T(8,128)(2,1)} %get-tuple-element.28), channel_id=1, source_target_pairs={{0,8},{8,16},{16,24},{1,9},{9,17},{17,25},{2,10},{10,18},{18,26},{... | collective-permute-start | bytes 786440 | tf_op jit(solution)/shard_map/ppermute | solution.py:302
  247.6 9.6 %collective-permute-start.14 = (bf16[2,256,256]{2,1,0:T(8,128)(2,1)}, bf16[2,256,256]{2,1,0:T(8,128)(2,1)}, u32[]{:S(2)}, u32[]{:S(2)}) collective-permute-start(bf16[2,256,256]{2,1,0:T(8,128)(2,1)} %get-tuple-element.30), channel_id=1, source_target_pairs={{0,8},{8,16},{16,24},{1,9},{9,17},{17,25},{2,10},{10,18},{18,26},{... | collective-permute-start | bytes 786440 | tf_op jit(solution)/shard_map/ppermute | solution.py:302
  265.8 10.1 %collective-permute-start.15 = (bf16[2,256,256]{2,1,0:T(8,128)(2,1)}, bf16[2,256,256]{2,1,0:T(8,128)(2,1)}, u32[]{:S(2)}, u32[]{:S(2)}) collective-permute-start(bf16[2,256,256]{2,1,0:T(8,128)(2,1)} %get-tuple-element.32), channel_id=1, source_target_pairs={{0,8},{8,16},{16,24},{1,9},{9,17},{17,25},{2,10},{10,18},{18,26},{... | collective-permute-start | bytes 786440 | tf_op jit(solution)/shard_map/ppermute | solution.py:302
  (3 other events, 2.9 us)
where the time goes:
time: 286 us; the launch traced here: 284 us
  waiting for transfers between devices  155 us (54%)
  Pallas kernels  62.2 us (22%)
  starting transfers between devices  30.4 us (11%)
  local copies, waits for them, and re-layouts  18.2 us (6%)
  other arithmetic  13.4 us (5%)
  between operations  5.56 us (2%)
    ppermute x3, waiting for transfers between devices, shards(): up_in = lax.ppermute(up_out, 'probe', up_route)  58.8 us
    ppermute x6, waiting for transfers between devices, shards(): carried = lax.ppermute(leaving, 'depth', forward)  56.6 us
    pallas_call x7, Pallas kernels, run_section(): pl.pallas_call(section_kernel, grid_spec=grid_spec, out_shape=[jax.ShapeD...  38.6 us
    ppermute x3, waiting for transfers between devices, shards(): down_in = lax.ppermute(down_out, 'probe', down_route)  25.6 us
    pallas_call x1, Pallas kernels, summed_atoms(): pl.pallas_call(functools.partial(sum_kernel, dests, tiles_dev), grid=(til...  23.6 us
    ppermute x3, starting transfers between devices, shards(): up_in = lax.ppermute(up_out, 'probe', up_route)  14.8 us
    convert_element_type x2, other arithmetic, shards(): up_out.astype(jnp.bfloat16)  7.96 us
    ppermute x6, starting transfers between devices, shards(): carried = lax.ppermute(leaving, 'depth', forward)  7.68 us
  transfers between devices with their start and end apart: 16, of which 13 were waited for; matrix products, arithmetic and copies ran while one was open for 5% of the time, Pallas kernels for 0%

commit v1 on v0

--- a/solution.py
+++ b/solution.py
@@ -47,24 +47,18 @@
     return 1.0 - 2.0 * sine * sine, 2.0 * sine * cosine
 
 
-def sum_kernel(dests, tiles_dev, where_ref, mine_ref, own_ref, other_ref, kept_ref, sent_ref, total):
+def sum_kernel(dests, tiles_dev, plan_ref, mine_ref, own_ref, other_ref, kept_ref, sent_ref, total):
     total[...] = jnp.zeros_like(total)
-    count = own_ref.shape[0]
-
-    def add_from(ref, base):
-        def body(atom, carry):
-            place = where_ref[base + atom]
-
-            @pl.when(place >= 0)
-            def _():
-                total[place] = total[place] + ref[atom].astype(jnp.float32)
-
+    def add_from(ref, source):
+        def body(entry, carry):
+            place = plan_ref[source, 1, entry]
+            total[place] = total[place] + ref[plan_ref[source, 0, entry]].astype(jnp.float32)
             return carry
 
-        lax.fori_loop(0, count, body, 0)
+        lax.fori_loop(0, mine_ref[1 + source], body, 0)
 
     add_from(own_ref, 0)
-    add_from(other_ref, count)
+    add_from(other_ref, 1)
     first = mine_ref[0] * tiles_dev
 
     def store_kept(tile, carry):
@@ -80,9 +74,9 @@
     lax.fori_loop(0, dests * tiles_dev, store_sent, 0)
 
 
-def summed_atoms(where, mine, own, other, dests, tiles_dev):
+def summed_atoms(plan, mine, own, other, dests, tiles_dev):
     tile_size = own.shape[-1]
-    rows = tile_size // 4
+    rows = tile_size // 2
     smem = pl.BlockSpec(memory_space=pltpu.SMEM)
 
     def part(array_count):
@@ -99,10 +93,11 @@
         out_specs=(part(tiles_dev), part(dests * tiles_dev)),
         scratch_shapes=[pltpu.VMEM((dests * tiles_dev, rows, tile_size), jnp.float32)],
         compiler_params=pltpu.CompilerParams(vmem_limit_bytes=VMEM_LIMIT),
-    )(where, mine, own, other)
+    )(plan, mine, own, other)
 
 
 def section_kernel(
+    step,
     info,
     launched,
     carried,
@@ -123,15 +118,15 @@
     wave,
 ):
     points = launched.shape[-1]
-    active = info[0] > 0
+    active = info[step, 0] > 0
 
     @pl.when(active)
     def _():
-        @pl.when(info[1] > 0)
+        @pl.when(info[step, 1] > 0)
         def _():
             wave[...] = launched[...].reshape(2 * points, points)
 
-        @pl.when(info[1] <= 0)
+        @pl.when(info[step, 1] <= 0)
         def _():
             wave[...] = carried[...].reshape(2 * points, points).astype(jnp.float32)
 
@@ -167,7 +162,7 @@
             wave[points:] = back_im
             return carry
 
-        lax.fori_loop(0, info[2], one_slice, 0)
+        lax.fori_loop(0, info[step, 2], one_slice, 0)
         out = wave[...].reshape(2, points, points)
         result[0] = out
         leaving[...] = out.astype(jnp.bfloat16)
@@ -178,7 +173,7 @@
         leaving[...] = jnp.zeros_like(leaving)
 
 
-def run_section(info, launched, carried, mid, above, below, tables, results):
+def run_section(step, info, launched, carried, mid, above, below, tables, results):
     points = launched.shape[-1]
     slots, _, tile_size, _ = mid.shape
     half = above.shape[2]
@@ -187,9 +182,9 @@
         return pl.BlockSpec(array.shape, lambda i, info, n=array.ndim: (0,) * n)
 
     def column(rows, which):
-        return pl.BlockSpec((slots, 1, rows, tile_size), lambda i, info: (0, info[which], 0, 0))
-
-    place = pl.BlockSpec((1, 2, points, points), lambda i, info: (info[5], 0, 0, 0))
+        return pl.BlockSpec((slots, 1, rows, tile_size), lambda i, info: (0, info[step, which], 0, 0))
+
+    place = pl.BlockSpec((1, 2, points, points), lambda i, info: (info[step, 5], 0, 0, 0))
     grid_spec = pltpu.PrefetchScalarGridSpec(
         num_scalar_prefetch=1,
         grid=(1,),
@@ -209,7 +204,7 @@
         scratch_shapes=[pltpu.VMEM((2 * points, points), jnp.float32)],
     )
     return pl.pallas_call(
-        section_kernel,
+        functools.partial(section_kernel, step),
         grid_spec=grid_spec,
         out_shape=[
             jax.ShapeDtypeStruct(results.shape, results.dtype),
@@ -235,10 +230,18 @@
     swap = [(i, i ^ 1) for i in range(owners)]
     other_blocks = lax.ppermute(blocks, "probe", swap)
     other_targets = lax.ppermute(targets, "probe", swap)
-    named = jnp.concatenate([targets, other_targets])
+    named = jnp.stack([targets, other_targets])
     owner_of = named // tiles_dev
-    where = jnp.where(owner_of % 2 == core, (owner_of // 2) * tiles_dev + named % tiles_dev, -1)
-    kept, sent = summed_atoms(where, rank[None], blocks, other_blocks, pairs, tiles_dev)
+    counts = owner_of % 2 == core
+    where = (owner_of // 2) * tiles_dev + named % tiles_dev
+    atom = jnp.arange(named.shape[1], dtype=jnp.int32)
+    earlier = counts[:, None, :] & (atom[None, :] < atom[:, None])[None]
+    order = jnp.sum(earlier.astype(jnp.int32), axis=2)
+    member = counts[:, None, :] & (order[:, None, :] == atom[None, :, None])
+    entries = jnp.stack([jnp.broadcast_to(atom[None], named.shape), where], axis=1)
+    plan = jnp.sum(jnp.where(member[:, None], entries[:, :, None, :], 0), axis=3)
+    mine = jnp.concatenate([rank[None], jnp.sum(counts.astype(jnp.int32), axis=1)])
+    kept, sent = summed_atoms(plan, mine, blocks, other_blocks, pairs, tiles_dev)
     sent = sent.reshape(pairs, tiles_dev, tile_size, tile_size)
 
     up_in = down_in = None
@@ -258,6 +261,7 @@
                 down_route.append((2 * (pairs - 1 - z) + c, 2 * (pairs - 2 - z) + c))
         up_in = lax.ppermute(up_out, "probe", up_route)
         down_in = lax.ppermute(down_out, "probe", down_route)
+        up_in, down_in = lax.optimization_barrier((up_in, down_in))
     if up_in is not None:
         kept = kept + up_in.astype(jnp.float32) + down_in.astype(jnp.float32)
     mid = reduced(kept).reshape(SLICE_MAX, TCOLS, tile_size, tile_size)
@@ -280,23 +284,25 @@
     carried = jnp.zeros(probe_wave.shape, jnp.bfloat16)
     forward = [(d, d + 1) for d in range(sections - 1)]
     step_total = waves_dev + sections - 1
+    wave_index = jnp.arange(step_total, dtype=jnp.int32) - depth_index
+    active = (wave_index >= 0) & (wave_index < waves_dev)
+    wave_index = jnp.clip(wave_index, 0, waves_dev - 1)
+    chosen = wave_index[:, None] == jnp.arange(waves_dev, dtype=jnp.int32)[None, :]
+    column = jnp.sum(jnp.where(chosen, positions[None, :], 0), axis=1)
+    info = jnp.stack(
+        [
+            active.astype(jnp.int32),
+            jnp.broadcast_to((depth_index == 0).astype(jnp.int32), active.shape),
+            jnp.broadcast_to(slice_counts[0], active.shape),
+            column,
+            (column + 1) % TCOLS,
+            wave_index,
+        ],
+        axis=1,
+    )
     for step in range(step_total):
-        wave_index = step - depth_index
-        active = (wave_index >= 0) & (wave_index < waves_dev)
-        wave_index = jnp.clip(wave_index, 0, waves_dev - 1)
-        column = positions[wave_index]
-        info = jnp.stack(
-            [
-                active.astype(jnp.int32),
-                (depth_index == 0).astype(jnp.int32),
-                slice_counts[0],
-                column,
-                (column + 1) % TCOLS,
-                wave_index,
-            ]
-        )
         results, leaving = run_section(
-            info, probe_wave, carried, mid, above, below, tables, results
+            step, info, probe_wave, carried, mid, above, below, tables, results
         )
         if step + 1 < step_total:
             carried = lax.ppermute(leaving, "depth", forward)

time: 286 us -> 248 us (0.87)
  Pallas kernels: 62.2 us -> 48.1 us
  waiting for transfers between devices: 155 us -> 141 us
  local copies, waits for them, and re-layouts: 18.2 us -> 6.54 us
  starting transfers between devices: 30.4 us -> 36.4 us
  between operations: 5.56 us -> 0.92 us
    ppermute x3, waiting for transfers between devices: 25.6 us -> 5.07 us  [shards(): down_in = lax.ppermute(down_out, 'probe', down_route)]
    pallas_call x1, Pallas kernels: 23.6 us -> 10.1 us  [summed_atoms(): pl.pallas_call(functools.partial(sum_kernel, dests, tiles_dev), grid=(til...]
    ppermute x6, waiting for transfers between devices: 56.6 us -> 67.3 us  [shards(): carried = lax.ppermute(leaving, 'depth', forward)]
    convert_element_type x2 -> x1, other arithmetic: 7.96 us -> 0.01 us  [shards(): active.astype(jnp.int32)]
    convert_element_type x1 -> x2, other arithmetic: 1.78 us -> 9.22 us  [shards(): down_out.astype(jnp.bfloat16)]
    ppermute x3, starting transfers between devices: 14.8 us -> 20.1 us  [shards(): up_in = lax.ppermute(up_out, 'probe', up_route)]
    another operation x7 -> x5, local copies, waits for them, and re-layouts: 5.08 us -> 0.19 us  [the longest x4 0.18 us: shards(): jnp.stack([active.astype(jnp.int32), jnp.broadcast_to((depth_index == 0)....]
    unnamed x22 -> x8, local copies, waits for them, and re-layouts: 5.91 us -> 1.09 us
  transfers between devices with their start and end apart: 16 -> 16, of which waited for: 13 -> 12; matrix products, arithmetic and copies ran while one was open for 5% -> 2% of each run, Pallas kernels for 0% -> 0%
where the time goes in v1:
time: 248 us
  waiting for transfers between devices  141 us (57%)
  Pallas kernels  48.1 us (19%)
  starting transfers between devices  36.4 us (15%)
  other arithmetic  15.7 us (6%)
  local copies, waits for them, and re-layouts  6.54 us (3%)
    ppermute x6, waiting for transfers between devices, shards(): carried = lax.ppermute(leaving, 'depth', forward)  67.3 us
    ppermute x3, waiting for transfers between devices, shards(): up_in = lax.ppermute(up_out, 'probe', up_route)  56.1 us
    pallas_call x7, Pallas kernels, run_section(): pl.pallas_call(functools.partial(section_kernel, step), grid_spec=grid_sp...  38 us
    ppermute x3, starting transfers between devices, shards(): up_in = lax.ppermute(up_out, 'probe', up_route)  20.1 us
    pallas_call x1, Pallas kernels, summed_atoms(): pl.pallas_call(functools.partial(sum_kernel, dests, tiles_dev), grid=(til...  10.1 us
    convert_element_type x2, other arithmetic, shards(): down_out.astype(jnp.bfloat16)  9.22 us
    ppermute x6, starting transfers between devices, shards(): carried = lax.ppermute(leaving, 'depth', forward)  7.68 us
    ppermute x1, waiting for transfers between devices, shards(): above = lax.ppermute(narrow[:, :, half_tile:], 'probe', up)  6.76 us
  transfers between devices with their start and end apart: 16, of which 12 were waited for; matrix products, arithmetic and copies ran while one was open for 2% of the time, Pallas kernels for 0%

profile of v1, /device:TPU:6, one launch (start us, length us, event | category | flops | bytes accessed | tf_op | source)
XLA Modules:
  0.0 248.3 jit_solution(7076355478058086023)
XLA Ops:
  0.6 5.5 %collective-permute-done = s32[128]{0:T(128)S(1)} collective-permute-done((s32[128]{0:T(128)}, s32[128]{0:T(128)S(1)}, u32[]{:S(2)}, u32[]{:S(2)}) %collective-permute-start) | collective-permute-done | bytes 544 | tf_op jit(solution)/shard_map/ppermute | solution.py:232
  7.9 10.1 %shard_map.64 = (f32[32,128,128]{2,1,0:T(8,128)S(1)}, bf16[128,128,128]{2,1,0:T(8,128)(2,1)}) custom-call(s32[2,2,128]{2,1,0:T(2,128)S(1)} %select_reduce_fusion.plan_ref, s32[3]{0:T(128)S(1)} %pad_add_fusion.3.mine_ref, bf16[128,128,128]{2,1,0:T(8,128)(2,1)} %bitcast.51, bf16[128,128,128]{2,1,0:T(8,128)(2,1)} %collective-permute-done.1.other_ref), custom_call_target="tpu_custom_call" | custom-call | tf_op jit(solution)/shard_map/pallas_call | solution.py:85
  18.0 2.7 %dynamic-slice_bitcast_fusion = (bf16[32,128,128]{2,1,0:T(8,128)(2,1)S(1)}, bf16[32,128,128]{2,1,0:T(8,128)(2,1)}) fusion(bf16[4,32,128,128]{3,2,1,0:T(8,128)(2,1)} %bitcast.47, s32[]{:T(128)S(6)} %min.38, s32[]{:T(128)S(6)} %min.37), kind=kLoop, calls=%fused_computation.9 | loop fusion | bytes 4194312 | tf_op jit(solution)/shard_map/jit(dynamic_index_in_dim)/squeeze | solution.py:252
  20.7 4.5 %collective-permute-start.2 = (bf16[32,128,128]{2,1,0:T(8,128)(2,1)}, bf16[32,128,128]{2,1,0:T(8,128)(2,1)}, u32[]{:S(2)}, u32[]{:S(2)}) collective-permute-start(bf16[32,128,128]{2,1,0:T(8,128)(2,1)} %get-tuple-element.54), channel_id=1, source_target_pairs={{0,2},{1,3},{8,10},{9,11},{16,18},{17,19},{24,26},{25,27}} | collective-permute-start | bytes 3145736 | tf_op jit(solution)/shard_map/ppermute | solution.py:262
  26.9 20.1 %collective-permute-done.2 = bf16[32,128,128]{2,1,0:T(8,128)(2,1)} collective-permute-done((bf16[32,128,128]{2,1,0:T(8,128)(2,1)}, bf16[32,128,128]{2,1,0:T(8,128)(2,1)}, u32[]{:S(2)}, u32[]{:S(2)}) %collective-permute-start.2) | collective-permute-done | bytes 1048608 | tf_op jit(solution)/shard_map/ppermute | solution.py:262
  47.0 4.3 %subtract_convert_fusion.2 = (bf16[32,128,128]{2,1,0:T(8,128)(2,1)S(1)}, bf16[32,128,128]{2,1,0:T(8,128)(2,1)}) fusion(bf16[32,128,128]{2,1,0:T(8,128)(2,1)} %collective-permute-done.3, bf16[4,32,128,128]{3,2,1,0:T(8,128)(2,1)} %bitcast.48, s32[]{:T(128)S(6)} %min.39, bf16[32,128,128]{2,1,0:T(8,128)(2,1)} %collective-permute-done.2, s32[]{:T(128)S(6)} %min.36), kind=kLoop, calls=%fused_computation.7 | loop fusion | flops 8388608 | bytes 6291464 | tf_op jit(solution)/shard_map/convert_element_type | solution.py:256
  51.4 5.3 %collective-permute-start.4 = (bf16[32,128,128]{2,1,0:T(8,128)(2,1)}, bf16[32,128,128]{2,1,0:T(8,128)(2,1)}, u32[]{:S(2)}, u32[]{:S(2)}) collective-permute-start(bf16[32,128,128]{2,1,0:T(8,128)(2,1)} %get-tuple-element.52), channel_id=1, source_target_pairs={{0,2},{1,3},{2,4},{3,5},{8,10},{9,11},{10,12},{11,13},{16,18},{17,... | collective-permute-start | bytes 3145736 | tf_op jit(solution)/shard_map/ppermute | solution.py:262
  58.3 19.3 %collective-permute-done.4 = bf16[32,128,128]{2,1,0:T(8,128)(2,1)} collective-permute-done((bf16[32,128,128]{2,1,0:T(8,128)(2,1)}, bf16[32,128,128]{2,1,0:T(8,128)(2,1)}, u32[]{:S(2)}, u32[]{:S(2)}) %collective-permute-start.4) | collective-permute-done | bytes 1048608 | tf_op jit(solution)/shard_map/ppermute | solution.py:262
  77.7 4.9 %subtract_convert_fusion = (bf16[32,128,128]{2,1,0:T(8,128)(2,1)}, bf16[32,128,128]{2,1,0:T(8,128)(2,1)}) fusion(bf16[32,128,128]{2,1,0:T(8,128)(2,1)} %collective-permute-done.5, bf16[4,32,128,128]{3,2,1,0:T(8,128)(2,1)} %bitcast.49, s32[]{:T(128)S(6)} %min.40, bf16[32,128,128]{2,1,0:T(8,128)(2,1)} %collective-permute-done.4, s32[]{:T(128)S(6)} %min.35), kind=kLoop, calls=%fused_computation.5 | loop fusion | flops 8388608 | bytes 6291464 | tf_op jit(solution)/shard_map/convert_element_type | solution.py:256
  82.6 10.2 %collective-permute-start.6 = (bf16[32,128,128]{2,1,0:T(8,128)(2,1)}, bf16[32,128,128]{2,1,0:T(8,128)(2,1)}, u32[]{:S(2)}, u32[]{:S(2)}) collective-permute-start(bf16[32,128,128]{2,1,0:T(8,128)(2,1)} %get-tuple-element.50), channel_id=1, source_target_pairs={{0,2},{1,3},{2,4},{3,5},{4,6},{5,7},{8,10},{9,11},{10,12},{11,13},... | collective-permute-start | bytes 3145736 | tf_op jit(solution)/shard_map/ppermute | solution.py:262
  96.3 16.6 %collective-permute-done.6 = bf16[32,128,128]{2,1,0:T(8,128)(2,1)} collective-permute-done((bf16[32,128,128]{2,1,0:T(8,128)(2,1)}, bf16[32,128,128]{2,1,0:T(8,128)(2,1)}, u32[]{:S(2)}, u32[]{:S(2)}) %collective-permute-start.6) | collective-permute-done | bytes 1048608 | tf_op jit(solution)/shard_map/ppermute | solution.py:262
  112.9 5.1 %collective-permute-done.7 = bf16[32,128,128]{2,1,0:T(8,128)(2,1)} collective-permute-done((bf16[32,128,128]{2,1,0:T(8,128)(2,1)}, bf16[32,128,128]{2,1,0:T(8,128)(2,1)}, u32[]{:S(2)}, u32[]{:S(2)}) %collective-permute-start.7) | collective-permute-done | bytes 1048608 | tf_op jit(solution)/shard_map/ppermute | solution.py:263
  121.4 3.5 %collective-permute-start.9 = (bf16[4,8,64,128]{3,2,1,0:T(8,128)(2,1)S(1)}, bf16[4,8,64,128]{3,2,1,0:T(8,128)(2,1)S(1)}, u32[]{:S(2)}, u32[]{:S(2)}) collective-permute-start(bf16[4,8,64,128]{3,2,1,0:T(8,128)(2,1)S(1)} %get-tuple-element.55), channel_id=1, source_target_pairs={{1,0},{2,1},{3,2},{4,3},{5,4},{6,5},{7,6},{0,7},{9,8},{10,9},{11,1... | collective-permute-start | bytes 1572872 | tf_op jit(solution)/shard_map/ppermute | solution.py:272
  127.0 6.8 %collective-permute-done.8.above_a.above_b = bf16[4,8,64,128]{3,2,1,0:T(8,128)(2,1)S(1)} collective-permute-done((bf16[4,8,64,128]{3,2,1,0:T(8,128)(2,1)S(1)}, bf16[4,8,64,128]{3,2,1,0:T(8,128)(2,1)S(1)}, u32[]{:S(2)}, u32[]{:S(2)}) %collective-permute-start.8) | collective-permute-done | bytes 524320 | tf_op jit(solution)/shard_map/ppermute | solution.py:271
  139.3 9.4 %collective-permute-done.10.carried = bf16[2,256,256]{2,1,0:T(8,128)(2,1)S(1)} collective-permute-done((bf16[2,256,256]{2,1,0:T(8,128)(2,1)S(1)}, bf16[2,256,256]{2,1,0:T(8,128)(2,1)S(1)}, u32[]{:S(2)}, u32[]{:S(2)}) %collective-permute-start.10) | collective-permute-done | bytes 262176 | tf_op jit(solution)/shard_map/ppermute | solution.py:308
  152.6 10.5 %collective-permute-done.11.carried = bf16[2,256,256]{2,1,0:T(8,128)(2,1)S(1)} collective-permute-done((bf16[2,256,256]{2,1,0:T(8,128)(2,1)S(1)}, bf16[2,256,256]{2,1,0:T(8,128)(2,1)S(1)}, u32[]{:S(2)}, u32[]{:S(2)}) %collective-permute-start.11) | collective-permute-done | bytes 262176 | tf_op jit(solution)/shard_map/ppermute | solution.py:308
  167.1 18.3 %collective-permute-done.12.carried = bf16[2,256,256]{2,1,0:T(8,128)(2,1)S(1)} collective-permute-done((bf16[2,256,256]{2,1,0:T(8,128)(2,1)S(1)}, bf16[2,256,256]{2,1,0:T(8,128)(2,1)S(1)}, u32[]{:S(2)}, u32[]{:S(2)}) %collective-permute-start.12) | collective-permute-done | bytes 262176 | tf_op jit(solution)/shard_map/ppermute | solution.py:308
  185.4 7.5 %shard_map.68 = (f32[4,2,256,256]{3,2,1,0:T(8,128)}, bf16[2,256,256]{2,1,0:T(8,128)(2,1)S(1)}) custom-call(s32[7,6]{1,0:T(8,128)S(1)} %stack.35.info, f32[2,256,256]{2,1,0:T(8,128)S(1)} %copy-done, bf16[2,256,256]{2,1,0:T(8,128)(2,1)S(1)} %collective-permute-done.12.carried, f32[4,8,128,128]{3,2,1,0:T(8,128)} %bitcast.39, ...), custom_call_target="tpu_custom_call", output_to_operand_aliasing={{0}: (14, {})} | custom-call | tf_op jit(solution)/shard_map/pallas_call | solution.py:206
  194.1 10.4 %collective-permute-done.13.carried = bf16[2,256,256]{2,1,0:T(8,128)(2,1)S(1)} collective-permute-done((bf16[2,256,256]{2,1,0:T(8,128)(2,1)S(1)}, bf16[2,256,256]{2,1,0:T(8,128)(2,1)S(1)}, u32[]{:S(2)}, u32[]{:S(2)}) %collective-permute-start.13) | collective-permute-done | bytes 262176 | tf_op jit(solution)/shard_map/ppermute | solution.py:308
  204.5 7.5 %shard_map.69 = (f32[4,2,256,256]{3,2,1,0:T(8,128)}, bf16[2,256,256]{2,1,0:T(8,128)(2,1)S(1)}) custom-call(s32[7,6]{1,0:T(8,128)S(1)} %stack.35.info, f32[2,256,256]{2,1,0:T(8,128)S(1)} %copy-done, bf16[2,256,256]{2,1,0:T(8,128)(2,1)S(1)} %collective-permute-done.13.carried, f32[4,8,128,128]{3,2,1,0:T(8,128)} %bitcast.41, ...), custom_call_target="tpu_custom_call", output_to_operand_aliasing={{0}: (14, {})} | custom-call | tf_op jit(solution)/shard_map/pallas_call | solution.py:206
  213.3 9.5 %collective-permute-done.14.carried = bf16[2,256,256]{2,1,0:T(8,128)(2,1)S(1)} collective-permute-done((bf16[2,256,256]{2,1,0:T(8,128)(2,1)S(1)}, bf16[2,256,256]{2,1,0:T(8,128)(2,1)S(1)}, u32[]{:S(2)}, u32[]{:S(2)}) %collective-permute-start.14) | collective-permute-done | bytes 262176 | tf_op jit(solution)/shard_map/ppermute | solution.py:308
  222.8 7.5 %shard_map.70 = (f32[4,2,256,256]{3,2,1,0:T(8,128)}, bf16[2,256,256]{2,1,0:T(8,128)(2,1)S(1)}) custom-call(s32[7,6]{1,0:T(8,128)S(1)} %stack.35.info, f32[2,256,256]{2,1,0:T(8,128)S(1)} %copy-done, bf16[2,256,256]{2,1,0:T(8,128)(2,1)S(1)} %collective-permute-done.14.carried, f32[4,8,128,128]{3,2,1,0:T(8,128)} %bitcast.43, ...), custom_call_target="tpu_custom_call", output_to_operand_aliasing={{0}: (14, {})} | custom-call | tf_op jit(solution)/shard_map/pallas_call | solution.py:206
  231.6 9.2 %collective-permute-done.15.carried = bf16[2,256,256]{2,1,0:T(8,128)(2,1)S(1)} collective-permute-done((bf16[2,256,256]{2,1,0:T(8,128)(2,1)S(1)}, bf16[2,256,256]{2,1,0:T(8,128)(2,1)S(1)}, u32[]{:S(2)}, u32[]{:S(2)}) %collective-permute-start.15) | collective-permute-done | bytes 262176 | tf_op jit(solution)/shard_map/ppermute | solution.py:308
  240.7 7.6 %shard_map.71 = (f32[4,2,256,256]{3,2,1,0:T(8,128)}, bf16[2,256,256]{2,1,0:T(8,128)(2,1)}) custom-call(s32[7,6]{1,0:T(8,128)S(1)} %stack.35.info, f32[2,256,256]{2,1,0:T(8,128)S(1)} %copy-done, bf16[2,256,256]{2,1,0:T(8,128)(2,1)S(1)} %collective-permute-done.15.carried, f32[4,8,128,128]{3,2,1,0:T(8,128)} %bitcast.45, ...), custom_call_target="tpu_custom_call", output_to_operand_aliasing={{0}: (14, {})} | custom-call | tf_op jit(solution)/shard_map/pallas_call | solution.py:206
  (55 shorter events, 31.1 us)
Async XLA Ops:
  0.0 7.9 %collective-permute-start.1 = (bf16[128,128,128]{2,1,0:T(8,128)(2,1)}, bf16[128,128,128]{2,1,0:T(8,128)(2,1)}, u32[]{:S(2)}, u32[]{:S(2)}) collective-permute-start(bf16[128,128,128]{2,1,0:T(8,128)(2,1)} %bitcast.50), channel_id=1, source_target_pairs={{0,1},{1,0},{2,3},{3,2},{4,5},{5,4},{6,7},{7,6},{8,9},{9,8},{10,11... | collective-permute-start | bytes 12582920 | tf_op jit(solution)/shard_map/ppermute | solution.py:231
  0.0 6.0 %collective-permute-start = (s32[128]{0:T(128)}, s32[128]{0:T(128)S(1)}, u32[]{:S(2)}, u32[]{:S(2)}) collective-permute-start(s32[128]{0:T(128)} %bitcast.52), channel_id=1, source_target_pairs={{0,1},{1,0},{2,3},{3,2},{4,5},{5,4},{6,7},{7,6},{8,9},{9,8},{10,11... | collective-permute-start | bytes 1544 | tf_op jit(solution)/shard_map/ppermute | solution.py:232
  20.7 26.3 %collective-permute-start.2 = (bf16[32,128,128]{2,1,0:T(8,128)(2,1)}, bf16[32,128,128]{2,1,0:T(8,128)(2,1)}, u32[]{:S(2)}, u32[]{:S(2)}) collective-permute-start(bf16[32,128,128]{2,1,0:T(8,128)(2,1)} %get-tuple-element.54), channel_id=1, source_target_pairs={{0,2},{1,3},{8,10},{9,11},{16,18},{17,19},{24,26},{25,27}} | collective-permute-start | bytes 3145736 | tf_op jit(solution)/shard_map/ppermute | solution.py:262
  25.2 21.8 %collective-permute-start.3 = (bf16[32,128,128]{2,1,0:T(8,128)(2,1)S(1)}, bf16[32,128,128]{2,1,0:T(8,128)(2,1)}, u32[]{:S(2)}, u32[]{:S(2)}) collective-permute-start(bf16[32,128,128]{2,1,0:T(8,128)(2,1)S(1)} %get-tuple-element.53), channel_id=1, source_target_pairs={{6,4},{7,5},{14,12},{15,13},{22,20},{23,21},{30,28},{31,29}} | collective-permute-start | bytes 3145736 | tf_op jit(solution)/shard_map/ppermute | solution.py:263
  51.4 26.3 %collective-permute-start.4 = (bf16[32,128,128]{2,1,0:T(8,128)(2,1)}, bf16[32,128,128]{2,1,0:T(8,128)(2,1)}, u32[]{:S(2)}, u32[]{:S(2)}) collective-permute-start(bf16[32,128,128]{2,1,0:T(8,128)(2,1)} %get-tuple-element.52), channel_id=1, source_target_pairs={{0,2},{1,3},{2,4},{3,5},{8,10},{9,11},{10,12},{11,13},{16,18},{17,... | collective-permute-start | bytes 3145736 | tf_op jit(solution)/shard_map/ppermute | solution.py:262
  56.7 21.0 %collective-permute-start.5 = (bf16[32,128,128]{2,1,0:T(8,128)(2,1)S(1)}, bf16[32,128,128]{2,1,0:T(8,128)(2,1)}, u32[]{:S(2)}, u32[]{:S(2)}) collective-permute-start(bf16[32,128,128]{2,1,0:T(8,128)(2,1)S(1)} %get-tuple-element.51), channel_id=1, source_target_pairs={{6,4},{7,5},{4,2},{5,3},{14,12},{15,13},{12,10},{13,11},{22,20},{2... | collective-permute-start | bytes 3145736 | tf_op jit(solution)/shard_map/ppermute | solution.py:263
  58.3 35.8 %copy-start.3 = (s32[4]{0:T(128)S(1)}, s32[4]{0:T(128)}, u32[]{:S(2)}) copy-start(s32[4]{0:T(128)} %param.9) | copy-start | bytes 52
  58.3 37.0 %copy-start.2 = (f32[256,256]{1,0:T(8,128)S(1)}, f32[256,256]{1,0:T(8,128)}, u32[]{:S(2)}) copy-start(f32[256,256]{1,0:T(8,128)} %param.11) | copy-start | bytes 786436
  82.6 30.3 %collective-permute-start.6 = (bf16[32,128,128]{2,1,0:T(8,128)(2,1)}, bf16[32,128,128]{2,1,0:T(8,128)(2,1)}, u32[]{:S(2)}, u32[]{:S(2)}) collective-permute-start(bf16[32,128,128]{2,1,0:T(8,128)(2,1)} %get-tuple-element.50), channel_id=1, source_target_pairs={{0,2},{1,3},{2,4},{3,5},{4,6},{5,7},{8,10},{9,11},{10,12},{11,13},... | collective-permute-start | bytes 3145736 | tf_op jit(solution)/shard_map/ppermute | solution.py:262
  92.8 25.2 %collective-permute-start.7 = (bf16[32,128,128]{2,1,0:T(8,128)(2,1)}, bf16[32,128,128]{2,1,0:T(8,128)(2,1)}, u32[]{:S(2)}, u32[]{:S(2)}) collective-permute-start(bf16[32,128,128]{2,1,0:T(8,128)(2,1)} %get-tuple-element.49), channel_id=1, source_target_pairs={{6,4},{7,5},{4,2},{5,3},{2,0},{3,1},{14,12},{15,13},{12,10},{13,11... | collective-permute-start | bytes 3145736 | tf_op jit(solution)/shard_map/ppermute | solution.py:263
  120.1 1.3 copy-start.1
  121.4 12.4 %collective-permute-start.8 = (bf16[4,8,64,128]{3,2,1,0:T(8,128)(2,1)S(1)}, bf16[4,8,64,128]{3,2,1,0:T(8,128)(2,1)S(1)}, u32[]{:S(2)}, u32[]{:S(2)}) collective-permute-start(bf16[4,8,64,128]{3,2,1,0:T(8,128)(2,1)S(1)} %get-tuple-element.56), channel_id=1, source_target_pairs={{0,1},{1,2},{2,3},{3,4},{4,5},{5,6},{6,7},{7,0},{8,9},{9,10},{10,1... | collective-permute-start | bytes 1572872 | tf_op jit(solution)/shard_map/ppermute | solution.py:271
  121.4 12.4 %collective-permute-start.9 = (bf16[4,8,64,128]{3,2,1,0:T(8,128)(2,1)S(1)}, bf16[4,8,64,128]{3,2,1,0:T(8,128)(2,1)S(1)}, u32[]{:S(2)}, u32[]{:S(2)}) collective-permute-start(bf16[4,8,64,128]{3,2,1,0:T(8,128)(2,1)S(1)} %get-tuple-element.55), channel_id=1, source_target_pairs={{1,0},{2,1},{3,2},{4,3},{5,4},{6,5},{7,6},{0,7},{9,8},{10,9},{11,1... | collective-permute-start | bytes 1572872 | tf_op jit(solution)/shard_map/ppermute | solution.py:272
  126.9 8.4 %copy-start = (f32[2,256,256]{2,1,0:T(8,128)S(1)}, f32[2,256,256]{2,1,0:T(8,128)}, u32[]{:S(2)}) copy-start(f32[2,256,256]{2,1,0:T(8,128)} %launched.13) | copy-start | bytes 1572868
  138.0 10.6 %collective-permute-start.10 = (bf16[2,256,256]{2,1,0:T(8,128)(2,1)S(1)}, bf16[2,256,256]{2,1,0:T(8,128)(2,1)S(1)}, u32[]{:S(2)}, u32[]{:S(2)}) collective-permute-start(bf16[2,256,256]{2,1,0:T(8,128)(2,1)S(1)} %get-tuple-element.34), channel_id=1, source_target_pairs={{0,8},{8,16},{16,24},{1,9},{9,17},{17,25},{2,10},{10,18},{18,26},{... | collective-permute-start | bytes 786440 | tf_op jit(solution)/shard_map/ppermute | solution.py:308
  151.3 11.8 %collective-permute-start.11 = (bf16[2,256,256]{2,1,0:T(8,128)(2,1)S(1)}, bf16[2,256,256]{2,1,0:T(8,128)(2,1)S(1)}, u32[]{:S(2)}, u32[]{:S(2)}) collective-permute-start(bf16[2,256,256]{2,1,0:T(8,128)(2,1)S(1)} %get-tuple-element.36), channel_id=1, source_target_pairs={{0,8},{8,16},{16,24},{1,9},{9,17},{17,25},{2,10},{10,18},{18,26},{... | collective-permute-start | bytes 786440 | tf_op jit(solution)/shard_map/ppermute | solution.py:308
  165.8 19.6 %collective-permute-start.12 = (bf16[2,256,256]{2,1,0:T(8,128)(2,1)S(1)}, bf16[2,256,256]{2,1,0:T(8,128)(2,1)S(1)}, u32[]{:S(2)}, u32[]{:S(2)}) collective-permute-start(bf16[2,256,256]{2,1,0:T(8,128)(2,1)S(1)} %get-tuple-element.38), channel_id=1, source_target_pairs={{0,8},{8,16},{16,24},{1,9},{9,17},{17,25},{2,10},{10,18},{18,26},{... | collective-permute-start | bytes 786440 | tf_op jit(solution)/shard_map/ppermute | solution.py:308
  192.9 11.7 %collective-permute-start.13 = (bf16[2,256,256]{2,1,0:T(8,128)(2,1)S(1)}, bf16[2,256,256]{2,1,0:T(8,128)(2,1)S(1)}, u32[]{:S(2)}, u32[]{:S(2)}) collective-permute-start(bf16[2,256,256]{2,1,0:T(8,128)(2,1)S(1)} %get-tuple-element.40), channel_id=1, source_target_pairs={{0,8},{8,16},{16,24},{1,9},{9,17},{17,25},{2,10},{10,18},{18,26},{... | collective-permute-start | bytes 786440 | tf_op jit(solution)/shard_map/ppermute | solution.py:308
  212.0 10.8 %collective-permute-start.14 = (bf16[2,256,256]{2,1,0:T(8,128)(2,1)S(1)}, bf16[2,256,256]{2,1,0:T(8,128)(2,1)S(1)}, u32[]{:S(2)}, u32[]{:S(2)}) collective-permute-start(bf16[2,256,256]{2,1,0:T(8,128)(2,1)S(1)} %get-tuple-element.42), channel_id=1, source_target_pairs={{0,8},{8,16},{16,24},{1,9},{9,17},{17,25},{2,10},{10,18},{18,26},{... | collective-permute-start | bytes 786440 | tf_op jit(solution)/shard_map/ppermute | solution.py:308
  230.3 10.5 %collective-permute-start.15 = (bf16[2,256,256]{2,1,0:T(8,128)(2,1)S(1)}, bf16[2,256,256]{2,1,0:T(8,128)(2,1)S(1)}, u32[]{:S(2)}, u32[]{:S(2)}) collective-permute-start(bf16[2,256,256]{2,1,0:T(8,128)(2,1)S(1)} %get-tuple-element.44), channel_id=1, source_target_pairs={{0,8},{8,16},{16,24},{1,9},{9,17},{17,25},{2,10},{10,18},{18,26},{... | collective-permute-start | bytes 786440 | tf_op jit(solution)/shard_map/ppermute | solution.py:308
